TPU v7x, 1024 devices: a whole 4x8x16 slice. The times are simulated.
1024 devices in a mesh: dp: 64 (over y, z_lo), fsdp: 16 (over z_hi, x, core).
Axes of the slice: x: 4, y: 8, z: 16 (z_hi: 2, z_lo: 8; z = z_hi * 8 + z_lo), core: 2. Of those that a mesh axis runs over, the one named last changes fastest.
Arguments:
- expert_weights: bfloat16 [16, 896, 896], P(None, 'fsdp'), may hold values from -0.1875 to 0.1875
- coefficients: float32 [1024, 16], replicated, may hold values from 0.05 to 1
- edge_inputs: bfloat16 [1024, 512, 896], P(('dp', 'fsdp')), may hold values from -6 to 6
- node_cotangent: bfloat16 [1024, 128, 896], P(('dp', 'fsdp')), may hold values from -6 to 6
- rotations: float32 [1024, 7, 7, 512], P(('dp', 'fsdp')), may hold values from -2 to 2
- targets: int32 [1024, 512], P(('dp', 'fsdp')), may hold values from 0 to 127
- counts: int32 [1024], P(('dp', 'fsdp')), may hold values from 128 to 512, as said below
Outputs:
- edge_grads: bfloat16 [1024, 512, 896], P(('dp', 'fsdp'))
- expert_grads: float32 [16, 896, 896], P(None, 'fsdp', 'dp')
Inputs may be any that keep to these rules, and one draw needn't show every extreme that they name: `counts`: a multiple of 128; some system has 512 live edges and some has 128.
All inputs are finite; a program needn't handle non-finite values.
Results may differ from a plain program's by a relative error of at most 0.0058.
Values may be sent and summed in bfloat16 or wider, within the bound.
A program may use at most 64 MiB of HBM per device.

v0:
```python
import jax
import jax.numpy as jnp
from jax import lax
from jax.sharding import PartitionSpec as P

L0 = 7


def per_device(
    expert_weights, coefficients, edge_inputs, node_cotangent, rotations, targets, counts
):
    groups = lax.axis_size("fsdp")
    experts, rows, width = expert_weights.shape
    edges = edge_inputs.shape[1]
    channels = width // L0
    group_idx = lax.axis_index("dp")
    group_coef = lax.dynamic_slice_in_dim(coefficients, group_idx * groups, groups, 0)
    wide = expert_weights.reshape(experts, rows * width).astype(jnp.float32)
    partial_merged = jnp.dot(group_coef, wide, precision=lax.Precision.HIGHEST)
    partial_merged = partial_merged.reshape(groups, rows, width).astype(jnp.bfloat16)
    merged = lax.all_to_all(partial_merged, "fsdp", split_axis=0, concat_axis=1, tiled=True)[0]
    slots = jnp.arange(edges, dtype=jnp.int32)
    live = (slots < counts[0]).astype(jnp.float32)
    picked = node_cotangent[0][targets[0]].reshape(edges, L0, channels).astype(jnp.float32)
    turned = jnp.einsum("abi,ibc->iac", rotations[0], picked, precision=lax.Precision.HIGHEST)
    rotated = (turned * live[:, None, None]).reshape(edges, width).astype(jnp.bfloat16)
    weight_grad = lax.dot_general(
        edge_inputs[0], rotated, (((0,), (0,)), ((), ())), preferred_element_type=jnp.float32
    )
    weight_grad = weight_grad.astype(jnp.bfloat16)
    grads = lax.dot_general(
        rotated, merged, (((1,), (1,)), ((), ())), preferred_element_type=jnp.float32
    )
    edge_grads = grads.astype(jnp.bfloat16)[None]
    pieces = lax.all_to_all(
        weight_grad.reshape(groups, rows, width), "fsdp", split_axis=0, concat_axis=0, tiled=True
    )
    flat = pieces.reshape(groups, rows * width).astype(jnp.float32)
    partial_value = jnp.dot(group_coef.T, flat, precision=lax.Precision.HIGHEST).reshape(
        experts, rows, width
    )
    expert_grads = lax.psum_scatter(partial_value, "dp", scatter_dimension=2, tiled=True)
    return (edge_grads, expert_grads)


def solution(mesh):
    placed = (
        P(None, "fsdp", None),
        P(),
        P(("dp", "fsdp"), None, None),
        P(("dp", "fsdp"), None, None),
        P(("dp", "fsdp"), None, None, None),
        P(("dp", "fsdp"), None),
        P(("dp", "fsdp")),
    )
    return jax.shard_map(
        per_device,
        mesh=mesh,
        in_specs=placed,
        out_specs=(P(("dp", "fsdp"), None, None), P(None, "fsdp", "dp")),
        check_vma=False,
    )
```

profile of v0, /device:TPU:36, one launch (start us, length us, event | category | flops | bytes accessed | tf_op | source)
XLA Modules:
  0.0 677.1 jit_solution(3679987554232954670)
XLA Ops:
  7.2 0.0 copy-start
  7.9 0.7 compare_select_fusion
  8.6 3.5 gather_fusion
  12.1 0.0 copy-start.2
  12.1 0.5 copy.23
  12.7 1.5 copy.24
  14.1 0.0 copy-done.2
  14.1 0.8 copy.34
  14.9 4.2 fusion.9
  19.1 1.6 copy.26
  20.8 0.0 copy-done
  20.8 2.3 convolution_convert_fusion
  23.1 21.7 %all-to-all-start.1 = ((bf16[16,56,896]{2,1,0:T(8,128)(2,1)}), bf16[16,56,896]{2,1,0:T(8,128)(2,1)S(1)}, u32[]{:S(2)}, u32[]{:S(2)}) async-start(bf16[16,56,896]{2,1,0:T(8,128)(2,1)} %bitcast.64), calls=%async_computation.1 | async-start | bytes 3211264 | tf_op jit(solution)/shard_map/all_to_all | solution.py:35
  44.8 0.0 reduce-scatter.2.cloned.1.call-start
  44.9 29.4 %all-to-all-done.1 = bf16[16,56,896]{2,1,0:T(8,128)(2,1)S(1)} async-done(((bf16[16,56,896]{2,1,0:T(8,128)(2,1)}), bf16[16,56,896]{2,1,0:T(8,128)(2,1)S(1)}, u32[]{:S(2)}, u32[]{:S(2)}) %all-to-all-start.1) | async-done | bytes 1605664 | tf_op jit(solution)/shard_map/all_to_all | solution.py:35
  74.2 3.9 fusion.4
  78.1 8.1 %copy.32 = f32[16,56,896]{1,0,2:T(8,128)} copy(f32[16,56,896]{2,0,1:T(8,128)} %fusion.4) | data formatting | bytes 6422528 | tf_op jit(solution)/shard_map/dot_general | solution.py:39
  86.2 0.0 copy-start.1
  86.2 0.0 reduce-scatter.2.cloned.1.call-update
  86.2 1.4 copy-done.1
  87.6 2.2 convolution_convert_fusion.1
  89.9 0.3 copy.29
  90.2 53.0 %all_to_all.14 = bf16[16,56,896]{2,1,0:T(8,128)(2,1)S(1)} all-to-all(bf16[16,56,896]{2,1,0:T(8,128)(2,1)S(1)} %copy.29), channel_id=1, replica_groups=mesh['dp'=64,'fsdp'=16] {'fsdp'}, dimensions={0} | all-to-all | bytes 3211264 | tf_op jit(solution)/shard_map/all_to_all | solution.py:21
  143.2 2.2 fusion.12
  145.4 524.9 %reduce-scatter.2.cloned.1.call-done = f32[16,56,14]{1,0,2:T(8,128)} async-done(((f32[16,56,896]{1,0,2:T(8,128)}), f32[16,56,14]{1,0,2:T(8,128)}) %reduce-scatter.2.cloned.1.call-update) | async-done | bytes 50192 | tf_op jit(solution)/shard_map/reduce_scatter | solution.py:42
  (2 shorter events, 0.0 us)
Async XLA Ops:
  7.2 13.6 %copy-start = (bf16[1,512,896]{2,1,0:T(8,128)(2,1)S(1)}, bf16[1,512,896]{2,1,0:T(8,128)(2,1)}, u32[]{:S(2)}) copy-start(bf16[1,512,896]{2,1,0:T(8,128)(2,1)} %param.9) | copy-start | bytes 2752516
  12.1 2.0 copy-start.2
  23.1 51.1 %all-to-all-start.1 = ((bf16[16,56,896]{2,1,0:T(8,128)(2,1)}), bf16[16,56,896]{2,1,0:T(8,128)(2,1)S(1)}, u32[]{:S(2)}, u32[]{:S(2)}) async-start(bf16[16,56,896]{2,1,0:T(8,128)(2,1)} %bitcast.64), calls=%async_computation.1 | async-start | bytes 3211264 | tf_op jit(solution)/shard_map/all_to_all | solution.py:35
  44.8 625.5 %reduce-scatter.2.cloned.1.call-start = ((), (), s32[]{:S(2)}) async-start(), calls=%async_computation.3 | async-start | bytes 7454720 | tf_op jit(solution)/shard_map/reduce_scatter | solution.py:42
  86.2 1.4 copy-start.1
Sparse Core Ops, SparseCore 0:
  86.4 583.8 reduce-scatter.1
where the time goes:
time: 678 us; the launch traced here: 677 us
  waiting for transfers between devices  554 us (82%)
  blocking collectives  53 us (8%)
  starting transfers between devices  21.7 us (3%)
  local copies, waits for them, and re-layouts  17.7 us (3%)
  matrix products  14.8 us (2%)
  between operations  14.8 us (2%)
    reduce_scatter x1, waiting for transfers between devices, per_device(): lax.psum_scatter(partial_value, 'dp', scatter_dimension=2, tiled=True)  525 us
    all_to_all x1, blocking collectives, per_device(): lax.all_to_all(partial_merged, 'fsdp', split_axis=0, concat_axis=1, tiled...  53 us
    all_to_all x1, waiting for transfers between devices, per_device(): lax.all_to_all(weight_grad.reshape(groups, rows, width), 'fsdp', split_ax...  29.4 us
    all_to_all x1, starting transfers between devices, per_device(): lax.all_to_all(weight_grad.reshape(groups, rows, width), 'fsdp', split_ax...  21.7 us
  transfers between devices with their start and end apart: 2, of which 2 were waited for; matrix products, arithmetic and copies ran while one was open for 1% of the time, Pallas kernels for 0%

commit v1 on v0

v1 whole, which is shorter than its diff:
```python
import jax
import jax.numpy as jnp
from jax import lax
from jax.experimental import pallas as pl
from jax.experimental.pallas import tpu as pltpu
from jax.sharding import PartitionSpec as P

MESH = pl.DeviceIdType.MESH
F32, BF16 = jnp.float32, jnp.bfloat16
L0, CH, EDGES, ATOMS, K, EXPERTS = 7, 128, 512, 128, 896, 16
NX, NY, NZ, NZL = 4, 8, 16, 8
GROUP = 8
ROWS, COLS = 56, 14
QS = 4
HALF = COLS // 2


def onehot(shape, test):
    rows = lax.broadcasted_iota(jnp.int32, shape, 0)
    cols = lax.broadcasted_iota(jnp.int32, shape, 1)
    return jnp.where(test(rows, cols), 1.0, 0.0).astype(BF16)


def dot(a, b):
    return jnp.dot(a, b, preferred_element_type=F32)


def kernel(
    w_ref, coef_ref, ct_ref, in_ref, node_ref, rot_ref, tgt_ref, cnt_ref,
    eg_ref, xg_ref,
    picked, rot_t, rot_n, in_pad, mix, gs, gr, area, part, zs, zr, total, ys, yr,
    wo, ms, mr, mg,
    g_send, g_recv, g_self, z_send, z_recv, y_send, y_recv,
    w_send, w_recv, a_send, a_recv, m_send, m_recv, m_self,
):
    dp, fs = lax.axis_index("dp"), lax.axis_index("fsdp")
    y, zl = dp // NZL, dp % NZL
    zh, g = fs // GROUP, fs % GROUP
    z = zh * NZL + zl
    py, yq = y % 2, y // 2

    def at(g_to, y_to, z_to):
        return (y_to * NZL + z_to % NZL, (z_to // NZL) * GROUP + g_to)

    near = y + 1 - 2 * py
    far = (y + 7 + 2 * py) % NY
    mirror = NZ - 1 - z
    up, down = (z + 1) % NZ, (z + NZ - 1) % NZ

    def send(src, dst, ssem, rsem, to):
        return pltpu.make_async_remote_copy(
            src_ref=src, dst_ref=dst, send_sem=ssem, recv_sem=rsem, device_id=to, device_id_type=MESH
        )

    barrier = pltpu.get_barrier_semaphore()
    greeted = [at((g + k) % GROUP, y, z) for k in range(1, GROUP)]
    greeted += [at((g + k) % GROUP, near, z) for k in range(GROUP)]
    greeted += [at((g + k) % GROUP, far, z) for k in range(GROUP)]
    greeted += [at(g, y, mirror), at(g, y, up), at(g, y, down)]
    greeted += [at(g, (y + 2 * k) % NY, z) for k in range(1, QS)]
    for to in greeted:
        pl.semaphore_signal(barrier, inc=1, device_id=to, device_id_type=MESH)

    hot = jnp.where(
        lax.broadcasted_iota(jnp.int32, (ATOMS, EDGES), 0) == tgt_ref[...], 1.0, 0.0
    ).astype(BF16)
    for b in range(L0):
        picked[b * CH : (b + 1) * CH, :] = lax.dot_general(
            node_ref[:, b * CH : (b + 1) * CH], hot, (((0,), (0,)), ((), ())), preferred_element_type=F32
        )
    live = jnp.where(
        lax.broadcasted_iota(jnp.int32, (1, EDGES), 1) < cnt_ref[0], 1.0, 0.0
    )

    def turn(i, _):
        start = pl.multiple_of(i * 16, 16)
        for lo in range(0, EDGES, 256):
            lanes = slice(lo, lo + 256)
            cols = [picked[pl.ds(b * CH + start, 16), lanes] for b in range(L0)]
            for a in range(L0):
                acc = rot_ref[a, 0:1, lanes] * cols[0]
                for b in range(1, L0):
                    acc += rot_ref[a, b : b + 1, lanes] * cols[b]
                rot_t[pl.ds(a * CH + start, 16), lanes] = (acc * live[:, lanes]).astype(BF16)
        return 0

    lax.fori_loop(0, CH // 16, turn, 0)

    for h in range(GROUP):
        put = onehot(
            (K, 128),
            lambda r, l, h=h: (r == (l // 64) * (K // 2) + h * ROWS + l % 64) & (l % 64 < ROWS),
        )
        in_pad[:, h * 128 : (h + 1) * 128] = dot(in_ref[...], put).astype(BF16)

    spread = onehot((256, 16), lambda m, e: m % 16 == e)
    gather = onehot((16, 256), lambda s, k: k // 16 == s)
    same = onehot((256, 256), lambda m, k: m // 16 == k % 16).astype(F32)
    for pair in range(2):
        coef = ct_ref[pair]
        high = coef.astype(BF16)
        low = (coef - high.astype(F32)).astype(BF16)
        for n, piece in enumerate((high, low)):
            wide = dot(dot(spread, piece).astype(BF16), gather)
            mix[pair, n] = (wide * same).astype(BF16)

    pl.semaphore_wait(barrier, len(greeted))

    w_copy = send(w_ref.at[y], wo.at[y], w_send.at[0], w_recv.at[0], at(g, y, mirror))
    w_copy.start()

    def g_copies(q, other):
        out = []
        for k in range(GROUP):
            g_to = (g + k) % GROUP
            if k > 0:
                out.append(send(
                    gs.at[q, py, g_to], gr.at[q, g], g_send.at[q, k], g_recv.at[q, k], at(g_to, y, z)
                ))
            out.append(send(
                gs.at[q, 1 - py, g_to], gr.at[q, GROUP + g],
                g_send.at[q, GROUP + k], g_recv.at[q, GROUP + k], at(g_to, other, z),
            ))
        return out

    def g_own(q):
        return pltpu.make_async_copy(gs.at[q, py, g], gr.at[q, g], g_self.at[q])

    def grad_chunk(q, other):
        for p in range(2):
            rows = rot_t[(2 * q + p) * 112 : (2 * q + p + 1) * 112, :]
            for h in range(0, GROUP, 2):
                block = dot(rows, in_pad[:, h * 128 : (h + 2) * 128]).astype(BF16)
                gs[q, p, h] = block[:, :128]
                gs[q, p, h + 1] = block[:, 128:]
        g_own(q).start()
        for copy in g_copies(q, other):
            copy.start()

    others = [near, near, far, far]
    for q in range(QS):
        grad_chunk(q, others[q])
    rot_n[...] = rot_t[...].T

    low_lanes = lax.broadcasted_iota(jnp.int32, (16, 128), 1) < 64

    def swap(v):
        return pltpu.roll(v, 64, 1)

    def contract(q):
        g_own(q).wait()
        for copy in g_copies(q, others[q]):
            copy.wait_recv()
        for t in range(7):
            block = gr[q, :, t * 16 : (t + 1) * 16, :].reshape(256, 128)
            made = dot(mix[q // 2, 0], block) + dot(mix[q // 2, 1], block)
            area[t * 16 : (t + 1) * 16] = made.reshape(16, 16, 128)

        def pack(i, _):
            for k in range(HALF):
                first, second = area[i * COLS + k], area[i * COLS + HALF + k]
                part[q, i, k] = jnp.where(low_lanes, first, swap(second))
                part[q, NZL + i, k] = jnp.where(low_lanes, swap(first), second)
            return 0

        lax.fori_loop(0, NZL, pack, 0)

    def steps(q, way):
        return 8 if way == q % 2 else 7

    def z_copy(q, way, s):
        return send(
            zs.at[q, way, s], zr.at[q, way, s], z_send.at[q, way, s], z_recv.at[q, way, s],
            at(g, y, up if way == 0 else down),
        )

    def ring_step(q, s):
        for way in range(2):
            n = steps(q, way)
            if s >= n:
                continue
            ahead = n - s
            owner = (z + ahead) % NZ if way == 0 else (z + NZ - ahead) % NZ
            value = part[q, owner]
            if s > 0:
                z_copy(q, way, s - 1).wait_recv()
                value += zr[q, way, s - 1].astype(F32)
            zs[q, way, s] = value.astype(BF16)
            z_copy(q, way, s).start()

    def ring_end(q):
        value = part[q, z]
        for way in range(2):
            n = steps(q, way)
            z_copy(q, way, n - 1).wait_recv()
            value += zr[q, way, n - 1].astype(F32)
        total[q] = value

    def m_copies(side):
        slot = (zh if side == 0 else 1 - zh) * GROUP + g
        return [
            send(
                ms.at[side, (g + k) % GROUP], mr.at[slot], m_send.at[side, k], m_recv.at[side, k],
                at((g + k) % GROUP, y, z),
            )
            for k in range(1, GROUP)
        ]

    def m_own(side):
        slot = (zh if side == 0 else 1 - zh) * GROUP + g
        return pltpu.make_async_copy(ms.at[side, g], mr.at[slot], m_self.at[side])

    def merge(side, source):
        tail = jnp.zeros((8, 128), F32)

        def block(i, _):
            lanes = pl.ds(pl.multiple_of(i * 128, 128), 128)
            for first in range(0, GROUP, 4):
                sums = [jnp.zeros((ROWS, 128), F32) for _ in range(4)]
                for e in range(0, EXPERTS, 2):
                    both = source[e // 2, :, lanes].astype(F32)
                    for j in range(4):
                        sums[j] += coef_ref[first + j, e] * both[:ROWS]
                        sums[j] += coef_ref[first + j, e + 1] * both[ROWS:]
                for j in range(4):
                    ms[side, first + j, :, lanes] = jnp.concatenate([sums[j], tail], 0).astype(BF16)
            return 0

        lax.fori_loop(0, K // 128, block, 0)
        m_own(side).start()
        for copy in m_copies(side):
            copy.start()

    def a_copy(way, s):
        piece = (y + NY - s) % NY if way == 0 else (y + s) % NY
        to = (y + 1) % NY if way == 0 else (y + NY - 1) % NY
        return send(wo.at[piece], wo.at[piece], a_send.at[way, s], a_recv.at[way, s], at(g, to, z))

    def a_came(way, s):
        piece = (y + NY - s - 1) % NY if way == 0 else (y + s + 1) % NY
        return send(wo.at[piece], wo.at[piece], a_send.at[way, s], a_recv.at[way, s], at(g, y, mirror))

    def gather_step(s):
        for way in range(2):
            if s >= 4 - way:
                continue
            if s > 0:
                a_came(way, s - 1).wait_recv()
            a_copy(way, s).start()

    done = [0] * QS

    def advance(q, count=1):
        for _ in range(count):
            if done[q] < 8:
                ring_step(q, done[q])
                done[q] += 1

    for q in range(QS):
        contract(q)
        advance(q)
        for before in range(q):
            advance(before, 2)
    merge(0, w_ref)
    w_copy.wait_recv()
    gather_step(0)
    for wave in range(7):
        for q in range(QS):
            advance(q)
        if wave in (1, 3, 5):
            gather_step(wave // 2 + 1)
    for q in range(QS):
        ring_end(q)

    def y_copy(k):
        q = (yq + k) % QS
        return send(ys.at[k], yr.at[k], y_send.at[k], y_recv.at[k], at(g, 2 * q + py, z))

    for k in range(1, QS):
        ys[k] = total[(yq + k) % QS].astype(BF16)
        y_copy(k).start()

    a_came(1, 2).wait_recv()
    a_came(0, 3).wait_recv()
    merge(1, wo)

    value = total[yq]
    for k in range(1, QS):
        y_copy(k).wait_recv()
        value += yr[k].astype(F32)
    for k in range(HALF):
        xg_ref[k] = value[k]
        xg_ref[HALF + k] = swap(value[k])

    for side in range(2):
        m_own(side).wait()
        for copy in m_copies(side):
            copy.wait_recv()
    for lo in range(0, K, 128):
        blocks = [mr[f, :, lo : lo + 128].astype(F32)[:ROWS] for f in range(2 * GROUP)]
        mg[:, lo : lo + 128] = jnp.concatenate(blocks, 0).astype(BF16)
    for lo in range(0, EDGES, 128):
        eg_ref[lo : lo + 128, :] = lax.dot_general(
            rot_n[lo : lo + 128, :], mg[...], (((1,), (1,)), ((), ())), preferred_element_type=F32
        ).astype(BF16)

    w_copy.wait_send()
    for q in range(QS):
        for copy in g_copies(q, others[q]):
            copy.wait_send()
        for way in range(2):
            for s in range(steps(q, way)):
                z_copy(q, way, s).wait_send()
    for k in range(1, QS):
        y_copy(k).wait_send()
    for way in range(2):
        for s in range(4 - way):
            a_copy(way, s).wait_send()
    for side in range(2):
        for copy in m_copies(side):
            copy.wait_send()


def per_device(
    expert_weights, coefficients, edge_inputs, node_cotangent, rotations, targets, counts
):
    dp, fs = lax.axis_index("dp"), lax.axis_index("fsdp")
    y, zl, zh = dp // NZL, dp % NZL, fs // GROUP

    def of_group(y_of):
        start = (y_of * NZL + zl) * (2 * GROUP) + zh * GROUP
        return lax.dynamic_slice_in_dim(coefficients, start, GROUP, 0)

    py = y % 2
    own = of_group(y)
    pairs = jnp.stack([
        jnp.concatenate([own, of_group(y + 1 - 2 * py)], 0).T,
        jnp.concatenate([own, of_group((y + 7 + 2 * py) % NY)], 0).T,
    ])
    vmem, smem = pl.BlockSpec(memory_space=pltpu.VMEM), pl.BlockSpec(memory_space=pltpu.SMEM)
    dma, shape = pltpu.SemaphoreType.DMA, pltpu.VMEM
    edge_grads, grads = pl.pallas_call(
        kernel,
        out_shape=(
            jax.ShapeDtypeStruct((EDGES, K), BF16),
            jax.ShapeDtypeStruct((COLS, EXPERTS, 128), F32),
        ),
        in_specs=[vmem, smem, vmem, vmem, vmem, vmem, vmem, smem],
        out_specs=(vmem, vmem),
        scratch_shapes=[
            shape((K, EDGES), F32),
            shape((K, EDGES), BF16),
            shape((EDGES, K), BF16),
            shape((EDGES, GROUP * 128), BF16),
            shape((2, 2, 256, 256), BF16),
            shape((QS, 2, GROUP, 112, 128), BF16),
            shape((QS, 2 * GROUP, 112, 128), BF16),
            shape((112, EXPERTS, 128), F32),
            shape((QS, NZ, HALF, EXPERTS, 128), F32),
            shape((QS, 2, 8, HALF, EXPERTS, 128), BF16),
            shape((QS, 2, 8, HALF, EXPERTS, 128), BF16),
            shape((QS, HALF, EXPERTS, 128), F32),
            shape((QS, HALF, EXPERTS, 128), BF16),
            shape((QS, HALF, EXPERTS, 128), BF16),
            shape((NY, 112, K), BF16),
            shape((2, GROUP, 64, K), BF16),
            shape((2 * GROUP, 64, K), BF16),
            shape((K, K), BF16),
            dma((QS, 16)), dma((QS, 16)), dma((QS,)),
            dma((QS, 2, 8)), dma((QS, 2, 8)),
            dma((QS,)), dma((QS,)),
            dma((1,)), dma((1,)),
            dma((2, 4)), dma((2, 4)),
            dma((2, GROUP)), dma((2, GROUP)), dma((2,)),
        ],
        compiler_params=pltpu.CompilerParams(
            collective_id=0, has_side_effects=True, vmem_limit_bytes=48 * 1024 * 1024
        ),
        name="edge_block_backward",
    )(
        expert_weights.reshape(NY, 112, K),
        own,
        pairs,
        edge_inputs[0],
        node_cotangent[0],
        rotations[0],
        targets,
        counts,
    )
    return edge_grads[None], jnp.transpose(grads[:, :, :ROWS], (1, 2, 0))


def solution(mesh):
    placed = (
        P(None, "fsdp", None),
        P(),
        P(("dp", "fsdp"), None, None),
        P(("dp", "fsdp"), None, None),
        P(("dp", "fsdp"), None, None, None),
        P(("dp", "fsdp"), None),
        P(("dp", "fsdp")),
    )
    return jax.shard_map(
        per_device,
        mesh=mesh,
        in_specs=placed,
        out_specs=(P(("dp", "fsdp"), None, None), P(None, "fsdp", "dp")),
        check_vma=False,
    )
```

time: 678 us -> 121 us (0.18)
  the two profiles are of different devices: /device:TPU:36 before, /device:TPU:7 now
where the time goes in v1:
time: 121 us; the launch traced here: 119 us
  Pallas kernels  110 us (91%)
  local copies, waits for them, and re-layouts  7.58 us (6%)
  between operations  1.39 us (1%)
    pallas_call x1, Pallas kernels, per_device(): pl.pallas_call(kernel, out_shape=(jax.ShapeDtypeStruct((EDGES, K), BF16),...  110 us
    unnamed x10, local copies, waits for them, and re-layouts  6.05 us

profile of v1, /device:TPU:7, one launch (start us, length us, event | category | flops | bytes accessed | tf_op | source)
XLA Modules:
  0.0 118.6 jit_solution(1653793383613489864)
XLA Ops:
  1.4 0.8 constant_dynamic-slice_fusion.1
  2.2 0.1 maximum_bitcast_fusion
  2.2 0.1 copy.9.coef_ref
  2.3 0.9 copy.12
  3.2 0.0 copy-start
  3.3 1.4 %copy-done = bf16[16,56,896]{2,1,0:T(8,128)(2,1)S(1)} copy-done((bf16[16,56,896]{2,1,0:T(8,128)(2,1)S(1)}, bf16[16,56,896]{2,1,0:T(8,128)(2,1)}, u32[]{:S(2)}) %copy-start) | copy-done | bytes 1605656
  4.7 0.0 copy-start.1
  4.7 1.2 copy-done.1
  5.8 0.0 copy-start.2
  5.8 0.9 copy-done.2
  6.8 0.0 copy-start.3
  6.8 0.7 copy-done.3
  7.5 109.5 %edge_block_backward.1 = (bf16[512,896]{1,0:T(8,128)(2,1)S(1)}, f32[14,16,128]{2,1,0:T(8,128)S(1)}) custom-call(bf16[8,112,896]{2,1,0:T(8,128)(2,1)S(1)} %bitcast.17, f32[8,16]{1,0:T(8,128)S(1)} %copy.9.coef_ref, f32[2,16,16]{2,1,0:T(8,128)S(1)} %pad_maximum_fusion.ct_ref, bf16[512,896]{1,0:T(8,128)(2,1)S(1)} %bitcast.19, bf16[128,896]{1,0:T(8,128)(2,1)S(1)} %bitcast.21, ...), custom_call_target="tpu_custom_call" | custom-call | tf_op jit(solution)/shard_map/edge_block_backward/pallas_call | solution.py:342
  117.0 0.7 slice_bitcast_fusion
  117.7 0.9 copy.15
  (1 shorter events, 0.0 us)
Async XLA Ops:
  3.2 1.4 %copy-start = (bf16[16,56,896]{2,1,0:T(8,128)(2,1)S(1)}, bf16[16,56,896]{2,1,0:T(8,128)(2,1)}, u32[]{:S(2)}) copy-start(bf16[16,56,896]{2,1,0:T(8,128)(2,1)} %param.7) | copy-start | bytes 4816900
  4.7 1.2 copy-start.1
  5.8 0.9 copy-start.2
  6.8 0.7 copy-start.3

commit v2 on v1

v2 whole, which is shorter than its diff:
```python
import jax
import jax.numpy as jnp
from jax import lax
from jax.experimental import pallas as pl
from jax.experimental.pallas import tpu as pltpu
from jax.sharding import PartitionSpec as P

MESH = pl.DeviceIdType.MESH
F32, BF16 = jnp.float32, jnp.bfloat16
L0, CH, EDGES, ATOMS, K, EXPERTS = 7, 128, 512, 128, 896, 16
NX, NY, NZ, NZL = 4, 8, 16, 8
GROUP = 8
ROWS, COLS = 56, 14
QS = 4
HALF = COLS // 2
OWN_AT = 0
FIRST_N = 4
OTHER_AT = ((4, 3), (5, 2), (6, 1), (7, 0), (), (), ())
LANES = K // 128


def onehot(shape, test):
    rows = lax.broadcasted_iota(jnp.int32, shape, 0)
    cols = lax.broadcasted_iota(jnp.int32, shape, 1)
    return jnp.where(test(rows, cols), 1.0, 0.0).astype(BF16)


def dot(a, b):
    return jnp.dot(a, b, preferred_element_type=F32)


def kernel(
    w_hbm, coef_ref, ct_ref, in_hbm, node_hbm, rot_hbm, tgt_ref, cnt_ref,
    eg_ref, xg_ref,
    w_ref, in_ref, node_ref, rot_ref, loads, picked, rot_t, rot_n, in_pad, mix, gs, gr, area, part, zs, zr, total, ys, yr,
    wo, ms, mo, mr, mg,
    g_send, g_recv, g_self, z_send, z_recv, y_send, y_recv,
    w_send, w_recv, o_send, o_recv, m_send, m_recv, m_self,
):
    dp, fs = lax.axis_index("dp"), lax.axis_index("fsdp")
    y, zl = lax.div(dp, NZL), lax.rem(dp, NZL)
    zh, g = lax.div(fs, GROUP), lax.rem(fs, GROUP)
    z = zh * NZL + zl
    py, yq = lax.rem(y, 2), lax.div(y, 2)

    def at(g_to, y_to, z_to):
        return (y_to * NZL + lax.rem(z_to, NZL), lax.div(z_to, NZL) * GROUP + g_to)

    near = y + 1 - 2 * py
    far = lax.rem(y + 7 + 2 * py, NY)
    mirror = NZ - 1 - z
    up, down = lax.rem(z + 1, NZ), lax.rem(z + NZ - 1, NZ)

    def send(src, dst, ssem, rsem, to):
        return pltpu.make_async_remote_copy(
            src_ref=src, dst_ref=dst, send_sem=ssem, recv_sem=rsem, device_id=to, device_id_type=MESH
        )

    load = [
        pltpu.make_async_copy(src, dst, loads.at[n])
        for n, (src, dst) in enumerate(
            ((node_hbm, node_ref), (rot_hbm, rot_ref), (in_hbm, in_ref), (w_hbm, w_ref))
        )
    ]
    for copy in load:
        copy.start()

    barrier = pltpu.get_barrier_semaphore()
    greeted = [
        at(lax.rem(g + k, GROUP), lax.rem(y + n, NY), z)
        for n in range(NY) for k in range(GROUP) if n + k > 0
    ]
    greeted += [at(g, y, mirror), at(g, y, up), at(g, y, down)]
    for to in greeted:
        pl.semaphore_signal(barrier, inc=1, device_id=to, device_id_type=MESH)

    hot = jnp.where(
        lax.broadcasted_iota(jnp.int32, (ATOMS, EDGES), 0) == tgt_ref[...], 1.0, 0.0
    ).astype(BF16)
    load[0].wait()
    for b in range(L0):
        picked[b * CH : (b + 1) * CH, :] = lax.dot_general(
            node_ref[:, b * CH : (b + 1) * CH], hot, (((0,), (0,)), ((), ())), preferred_element_type=F32
        )
    live = jnp.where(
        lax.broadcasted_iota(jnp.int32, (1, EDGES), 1) < cnt_ref[0], 1.0, 0.0
    )

    def turn(degrees):
        def rows(i, _):
            start = pl.multiple_of(i * 16, 16)
            for n in range(EDGES // 128):
                lanes = slice(n * 128, (n + 1) * 128)
                cols = [picked[pl.ds(b * CH + start, 16), lanes] for b in range(L0)]
                for a in degrees:
                    acc = None
                    for b in range(L0):
                        row = (a * L0 + b) * (EDGES // 128) + n
                        term = rot_ref[row : row + 1, :] * cols[b]
                        acc = term if acc is None else acc + term
                    rot_t[pl.ds(a * CH + start, 16), lanes] = (acc * live[:, lanes]).astype(BF16)
            return 0

        lax.fori_loop(0, CH // 16, rows, 0)

    load[1].wait()
    turn((0, 1))

    pl.semaphore_wait(barrier, len(greeted))

    own_lanes = pl.ds(pl.multiple_of(lax.rem(y, LANES) * 128, 128), 128)
    w_copy = send(
        w_hbm.at[:, :, own_lanes], wo, w_send.at[0], w_recv.at[0], at(g, y, mirror)
    )

    @pl.when(y < LANES)
    def _():
        w_copy.start()

    load[2].wait()
    for h in range(GROUP):
        block = None
        for half in range(2):
            first = half * (K // 2) + h * ROWS
            lo = first // 128 * 128
            hi = -(-(first + ROWS) // 128) * 128
            put = onehot(
                (hi - lo, 128),
                lambda r, l, half=half, d=first - lo: (r == d + l - half * 64)
                & (l >= half * 64) & (l < half * 64 + ROWS),
            )
            part_of = dot(in_ref[:, lo:hi], put)
            block = part_of if block is None else block + part_of
        in_pad[:, h * 128 : (h + 1) * 128] = block.astype(BF16)

    def g_copies(q, other):
        out = []
        for k in range(GROUP):
            g_to = lax.rem(g + k, GROUP)
            if k > 0:
                out.append(send(
                    gs.at[q, py, g_to], gr.at[q, g], g_send.at[q, k], g_recv.at[q, k], at(g_to, y, z)
                ))
            out.append(send(
                gs.at[q, 1 - py, g_to], gr.at[q, GROUP + g],
                g_send.at[q, GROUP + k], g_recv.at[q, GROUP + k], at(g_to, other, z),
            ))
        return out

    def g_own(q):
        return pltpu.make_async_copy(gs.at[q, py, g], gr.at[q, g], g_self.at[q])

    def grad_chunk(q, other):
        for p in range(2):
            rows = rot_t[(2 * q + p) * 112 : (2 * q + p + 1) * 112, :]
            for h in range(0, GROUP, 2):
                block = dot(rows, in_pad[:, h * 128 : (h + 2) * 128]).astype(BF16)
                gs[q, p, h] = block[:, :128]
                gs[q, p, h + 1] = block[:, 128:]
        g_own(q).start()
        for copy in g_copies(q, other):
            copy.start()

    others = [near, near, far, far]
    for q in range(QS):
        if q > 0:
            turn(((2, 3), (4, 5), (6,))[q - 1])
        grad_chunk(q, others[q])
    rot_n[...] = rot_t[...].T

    spread = onehot((256, 16), lambda m, e: m % 16 == e)
    gather = onehot((16, 256), lambda s, k: k // 16 == s)
    same = onehot((256, 256), lambda m, k: m // 16 == k % 16).astype(F32)
    for pair in range(2):
        coef = ct_ref[pair]
        high = coef.astype(BF16)
        low = (coef - high.astype(F32)).astype(BF16)
        for n, piece in enumerate((high, low)):
            wide = dot(dot(spread, piece).astype(BF16), gather)
            mix[pair, n] = (wide * same).astype(BF16)

    low_lanes = lax.broadcasted_iota(jnp.int32, (16, 128), 1) < 64

    def swap(v):
        return pltpu.roll(v, 64, 1)

    def contract(q):
        g_own(q).wait()
        for copy in g_copies(q, others[q]):
            copy.wait_recv()
        for t in range(7):
            block = gr[q, :, t * 16 : (t + 1) * 16, :].reshape(256, 128)
            made = dot(mix[q // 2, 0], block) + dot(mix[q // 2, 1], block)
            area[t * 16 : (t + 1) * 16] = made.reshape(16, 16, 128)

        def pack(i, _):
            for k in range(HALF):
                first, second = area[i * COLS + k], area[i * COLS + HALF + k]
                part[q, i, k] = jnp.where(low_lanes, first, swap(second))
                part[q, NZL + i, k] = jnp.where(low_lanes, swap(first), second)
            return 0

        lax.fori_loop(0, NZL, pack, 0)

    def steps(q, way):
        return 8 if way == q % 2 else 7

    def z_copy(q, way, s):
        return send(
            zs.at[q, way, s], zr.at[q, way, s], z_send.at[q, way, s], z_recv.at[q, way, s],
            at(g, y, up if way == 0 else down),
        )

    def ring_step(q, s):
        for way in range(2):
            n = steps(q, way)
            if s >= n:
                continue
            ahead = n - s
            owner = lax.rem(z + ahead, NZ) if way == 0 else lax.rem(z + NZ - ahead, NZ)
            value = part[q, owner]
            if s > 0:
                z_copy(q, way, s - 1).wait_recv()
                value += zr[q, way, s - 1].astype(F32)
            zs[q, way, s] = value.astype(BF16)
            z_copy(q, way, s).start()

    def ring_end(q):
        value = part[q, z]
        for way in range(2):
            n = steps(q, way)
            z_copy(q, way, n - 1).wait_recv()
            value += zr[q, way, n - 1].astype(F32)
        total[q] = value

    def m_copies():
        return [
            send(
                ms.at[lax.rem(g + k, GROUP)], mr.at[zh * GROUP + g], m_send.at[k], m_recv.at[k],
                at(lax.rem(g + k, GROUP), y, z),
            )
            for k in range(1, GROUP)
        ]

    def m_own():
        return pltpu.make_async_copy(ms.at[g], mr.at[zh * GROUP + g], m_self.at[0])

    tail = jnp.zeros((8, 128), F32)

    def mixed(first, source, lanes):
        sums = [None] * 4
        for e in range(0, EXPERTS, 2):
            both = source[e // 2, :, lanes].astype(F32)
            for j in range(4):
                term = coef_ref[first + j, e] * both[:ROWS] + coef_ref[first + j, e + 1] * both[ROWS:]
                sums[j] = term if e == 0 else sums[j] + term
        return [jnp.concatenate([v, tail], 0).astype(BF16) for v in sums]

    def merge_own():
        def block(i, _):
            lanes = pl.ds(pl.multiple_of(i * 128, 128), 128)
            for first in range(0, GROUP, 4):
                for j, v in enumerate(mixed(y * GROUP + first, w_ref, lanes)):
                    ms[first + j, i] = v
            return 0

        load[3].wait()
        lax.fori_loop(0, LANES, block, 0)
        m_own().start()
        for copy in m_copies():
            copy.start()

    def o_copies(n):
        return [
            send(
                mo.at[n, lax.rem(g + k, GROUP)], mr.at[(1 - zh) * GROUP + g, lax.rem(y, LANES)],
                o_send.at[n, k], o_recv.at[n, k], at(lax.rem(g + k, GROUP), lax.rem(y + n, NY), z),
            )
            for k in range(GROUP) if n + k > 0
        ]

    def o_own():
        return pltpu.make_async_copy(
            mo.at[0, g], mr.at[(1 - zh) * GROUP + g, lax.rem(y, LANES)], m_self.at[1]
        )

    def merge_other(n):
        @pl.when(y < LANES)
        def _():
            if n == FIRST_N:
                w_copy.wait_recv()
            for first in range(0, GROUP, 4):
                rows = lax.rem(y + n, NY) * GROUP + first
                for j, v in enumerate(mixed(rows, wo, slice(None))):
                    mo[n, first + j] = v
            if n == 0:
                o_own().start()
            for copy in o_copies(n):
                copy.start()

    def other_came(n):
        @pl.when(lax.rem(y + NY - n, NY) < LANES)
        def _():
            if n == 0:
                o_own().wait()
            for copy in o_copies(n):
                copy.wait_recv()

    def other_left(n):
        @pl.when(y < LANES)
        def _():
            for copy in o_copies(n):
                copy.wait_send()

    done = [0] * QS

    def advance(q, count=1):
        for _ in range(count):
            if done[q] < 8:
                ring_step(q, done[q])
                done[q] += 1

    for q in range(QS):
        if q == OWN_AT:
            merge_own()
        contract(q)
        advance(q)
        if q == 2:
            advance(0)
    for wave in range(7):
        if wave + QS == OWN_AT:
            merge_own()
        for n in OTHER_AT[wave]:
            merge_other(n)
        for q in range(QS):
            advance(q)
    for q in range(QS):
        ring_end(q)

    def y_copy(k):
        q = lax.rem(yq + k, QS)
        return send(ys.at[k], yr.at[k], y_send.at[k], y_recv.at[k], at(g, 2 * q + py, z))

    for k in range(1, QS):
        ys[k] = total[lax.rem(yq + k, QS)].astype(BF16)
        y_copy(k).start()

    m_own().wait()
    for copy in m_copies():
        copy.wait_recv()
    for n in range(NY):
        other_came(n)
    for i in range(LANES):
        blocks = [mr[f, i].astype(F32)[:ROWS] for f in range(2 * GROUP)]
        mg[:, i * 128 : (i + 1) * 128] = jnp.concatenate(blocks, 0).astype(BF16)
    for lo in range(0, EDGES, 128):
        eg_ref[lo : lo + 128, :] = lax.dot_general(
            rot_n[lo : lo + 128, :], mg[...], (((1,), (1,)), ((), ())), preferred_element_type=F32
        ).astype(BF16)

    value = total[yq]
    for k in range(1, QS):
        y_copy(k).wait_recv()
        value += yr[k].astype(F32)
    for k in range(HALF):
        xg_ref[k] = value[k]
        xg_ref[HALF + k] = swap(value[k])


    @pl.when(y < LANES)
    def _():
        w_copy.wait_send()

    for q in range(QS):
        for copy in g_copies(q, others[q]):
            copy.wait_send()
        for way in range(2):
            for s in range(steps(q, way)):
                z_copy(q, way, s).wait_send()
    for k in range(1, QS):
        y_copy(k).wait_send()
    for copy in m_copies():
        copy.wait_send()
    for n in range(NY):
        other_left(n)


def per_device(
    expert_weights, coefficients, edge_inputs, node_cotangent, rotations, targets, counts
):
    dp, fs = lax.axis_index("dp"), lax.axis_index("fsdp")
    y, zl, zh = lax.div(dp, NZL), lax.rem(dp, NZL), lax.div(fs, GROUP)

    grouped = coefficients.reshape(NY, NZL, 2, GROUP, EXPERTS)
    level = lax.dynamic_slice(grouped, (0, zl, zh, 0, 0), (NY, 1, 1, GROUP, EXPERTS))
    level = level.reshape(NY, GROUP, EXPERTS)

    def of_group(y_of):
        return lax.dynamic_slice_in_dim(level, y_of, 1, 0)[0]

    py = lax.rem(y, 2)
    own = of_group(y)
    pairs = jnp.stack([
        jnp.concatenate([own, of_group(y + 1 - 2 * py)], 0).T,
        jnp.concatenate([own, of_group(lax.rem(y + 7 + 2 * py, NY))], 0).T,
    ])
    vmem, smem = pl.BlockSpec(memory_space=pltpu.VMEM), pl.BlockSpec(memory_space=pltpu.SMEM)
    hbm = pl.BlockSpec(memory_space=pltpu.HBM)
    dma, shape = pltpu.SemaphoreType.DMA, pltpu.VMEM
    edge_grads, grads = pl.pallas_call(
        kernel,
        out_shape=(
            jax.ShapeDtypeStruct((EDGES, K), BF16),
            jax.ShapeDtypeStruct((COLS, EXPERTS, 128), F32),
        ),
        in_specs=[hbm, smem, vmem, hbm, hbm, hbm, vmem, smem],
        out_specs=(vmem, vmem),
        scratch_shapes=[
            shape((NY, 112, K), BF16),
            shape((EDGES, K), BF16),
            shape((ATOMS, K), BF16),
            shape((L0 * L0 * EDGES // 128, 128), F32),
            dma((4,)),
            shape((K, EDGES), F32),
            shape((K, EDGES), BF16),
            shape((EDGES, K), BF16),
            shape((EDGES, GROUP * 128), BF16),
            shape((2, 2, 256, 256), BF16),
            shape((QS, 2, GROUP, 112, 128), BF16),
            shape((QS, 2 * GROUP, 112, 128), BF16),
            shape((112, EXPERTS, 128), F32),
            shape((QS, NZ, HALF, EXPERTS, 128), F32),
            shape((QS, 2, 8, HALF, EXPERTS, 128), BF16),
            shape((QS, 2, 8, HALF, EXPERTS, 128), BF16),
            shape((QS, HALF, EXPERTS, 128), F32),
            shape((QS, HALF, EXPERTS, 128), BF16),
            shape((QS, HALF, EXPERTS, 128), BF16),
            shape((NY, 112, 128), BF16),
            shape((GROUP, LANES, 64, 128), BF16),
            shape((NY, GROUP, 64, 128), BF16),
            shape((2 * GROUP, LANES, 64, 128), BF16),
            shape((K, K), BF16),
            dma((QS, 16)), dma((QS, 16)), dma((QS,)),
            dma((QS, 2, 8)), dma((QS, 2, 8)),
            dma((QS,)), dma((QS,)),
            dma((1,)), dma((1,)),
            dma((NY, GROUP)), dma((NY, GROUP)),
            dma((GROUP,)), dma((GROUP,)), dma((2,)),
        ],
        compiler_params=pltpu.CompilerParams(
            collective_id=0, has_side_effects=True, vmem_limit_bytes=48 * 1024 * 1024
        ),
        name="edge_block_backward",
    )(
        expert_weights.reshape(NY, 112, K),
        level.reshape(NY * GROUP, EXPERTS),
        pairs,
        edge_inputs[0],
        node_cotangent[0],
        rotations.reshape(L0 * L0 * EDGES // 128, 128),
        targets,
        counts,
    )
    return edge_grads[None], jnp.transpose(grads[:, :, :ROWS], (1, 2, 0))


def solution(mesh):
    placed = (
        P(None, "fsdp", None),
        P(),
        P(("dp", "fsdp"), None, None),
        P(("dp", "fsdp"), None, None),
        P(("dp", "fsdp"), None, None, None),
        P(("dp", "fsdp"), None),
        P(("dp", "fsdp")),
    )
    return jax.shard_map(
        per_device,
        mesh=mesh,
        in_specs=placed,
        out_specs=(P(("dp", "fsdp"), None, None), P(None, "fsdp", "dp")),
        check_vma=False,
    )
```

time: 121 us -> 93.1 us (0.77); the launches traced: 119 us -> 92 us
  Pallas kernels: 110 us -> 83.4 us
  local copies, waits for them, and re-layouts: 7.58 us -> 5.91 us
    pallas_call x1, Pallas kernels: 110 us -> 83.4 us  [per_device(): pl.pallas_call(kernel, out_shape=(jax.ShapeDtypeStruct((EDGES, K), BF16),...]
where the time goes in v2:
time: 93.1 us; the launch traced here: 92 us
  Pallas kernels  83.4 us (90%)
  local copies, waits for them, and re-layouts  5.91 us (6%)
  between operations  1.47 us (2%)
  other arithmetic  1.22 us (1%)
    pallas_call x1, Pallas kernels, per_device(): pl.pallas_call(kernel, out_shape=(jax.ShapeDtypeStruct((EDGES, K), BF16),...  83.4 us
    unnamed x10, local copies, waits for them, and re-layouts  4.99 us

profile of v2, /device:TPU:7, one launch (start us, length us, event | category | flops | bytes accessed | tf_op | source)
XLA Modules:
  0.0 92.0 jit_solution(7501902973335351122)
XLA Ops:
  0.6 0.0 copy-start.1
  1.4 1.1 %reduce = f32[7,7,512]{2,1,0:T(8,128)S(1)} reduce(f32[1,7,7,512]{3,0,2,1:T(1,128)} %param.11, f32[]{:T(128)} %constant.111), dimensions={0}, to_apply=%param.11.reduce_sub_computation | reduce | bytes 200708 | tf_op args[4]
  2.6 1.0 %copy.9 = f32[1024,16]{1,0:T(8,128)S(1)} copy(f32[1024,16]{0,1:T(8,128)} %param.8) | data formatting | bytes 131072 | tf_op args[1]
  3.7 0.1 copy.11
  3.7 0.1 copy.13
  3.8 0.1 copy.10
  3.9 0.1 maximum_bitcast_fusion
  4.0 0.0 copy-done.1
  4.0 0.0 copy-start
  4.0 1.4 %copy-done = bf16[16,56,896]{2,1,0:T(8,128)(2,1)S(1)} copy-done((bf16[16,56,896]{2,1,0:T(8,128)(2,1)S(1)}, bf16[16,56,896]{2,1,0:T(8,128)(2,1)}, u32[]{:S(2)}) %copy-start) | copy-done | bytes 1605656
  5.4 0.0 copy-start.2
  5.4 0.9 %copy-done.2 = bf16[1,128,896]{2,1,0:T(8,128)(2,1)S(1)} copy-done((bf16[1,128,896]{2,1,0:T(8,128)(2,1)S(1)}, bf16[1,128,896]{2,1,0:T(8,128)(2,1)}, u32[]{:S(2)}) %copy-start.2) | copy-done | bytes 229400
  6.3 0.0 copy-start.3
  6.3 0.7 copy-done.3
  7.0 83.4 %edge_block_backward.1 = (bf16[512,896]{1,0:T(8,128)(2,1)S(1)}, f32[14,16,128]{2,1,0:T(8,128)S(1)}) custom-call(bf16[8,112,896]{2,1,0:T(8,128)(2,1)S(1)} %bitcast.23, f32[64,16]{1,0:T(8,128)S(1)} %dynamic-slice_bitcast_fusion.coef_ref, f32[2,16,16]{2,1,0:T(8,128)S(1)} %pad_maximum_fusion.ct_ref, bf16[512,896]{1,0:T(8,128)(2,1)S(1)} %bitcast.25, ...), custom_call_target="tpu_custom_call" | custom-call | tf_op jit(solution)/shard_map/edge_block_backward/pallas_call | solution.py:410
  90.5 0.7 slice_bitcast_fusion
  91.1 0.9 %copy.16 = bf16[1,512,896]{2,1,0:T(8,128)(2,1)} copy(bf16[1,512,896]{2,1,0:T(8,128)(2,1)S(1)} %bitcast.24) | data formatting | bytes 1835008
  (4 shorter events, 0.1 us)
Async XLA Ops:
  0.6 3.3 %copy-start.1 = (bf16[1,512,896]{2,1,0:T(8,128)(2,1)S(1)}, bf16[1,512,896]{2,1,0:T(8,128)(2,1)}, u32[]{:S(2)}) copy-start(bf16[1,512,896]{2,1,0:T(8,128)(2,1)} %param.9) | copy-start | bytes 2752516
  4.0 1.4 %copy-start = (bf16[16,56,896]{2,1,0:T(8,128)(2,1)S(1)}, bf16[16,56,896]{2,1,0:T(8,128)(2,1)}, u32[]{:S(2)}) copy-start(bf16[16,56,896]{2,1,0:T(8,128)(2,1)} %param.7) | copy-start | bytes 4816900
  5.4 0.9 %copy-start.2 = (bf16[1,128,896]{2,1,0:T(8,128)(2,1)S(1)}, bf16[1,128,896]{2,1,0:T(8,128)(2,1)}, u32[]{:S(2)}) copy-start(bf16[1,128,896]{2,1,0:T(8,128)(2,1)} %param.10) | copy-start | bytes 688132
  6.3 0.7 copy-start.3

commit v3 on v2

--- a/solution.py
+++ b/solution.py
@@ -96,7 +96,7 @@
                     acc = None
                     for b in range(L0):
                         row = (a * L0 + b) * (EDGES // 128) + n
-                        term = rot_ref[row : row + 1, :] * cols[b]
+                        term = rot_ref[a * L0 + b, n : n + 1, :] * cols[b]
                         acc = term if acc is None else acc + term
                     rot_t[pl.ds(a * CH + start, 16), lanes] = (acc * live[:, lanes]).astype(BF16)
             return 0
@@ -419,7 +419,7 @@
             shape((NY, 112, K), BF16),
             shape((EDGES, K), BF16),
             shape((ATOMS, K), BF16),
-            shape((L0 * L0 * EDGES // 128, 128), F32),
+            shape((L0 * L0, EDGES // 128, 128), F32),
             dma((4,)),
             shape((K, EDGES), F32),
             shape((K, EDGES), BF16),
@@ -448,7 +448,7 @@
             dma((GROUP,)), dma((GROUP,)), dma((2,)),
         ],
         compiler_params=pltpu.CompilerParams(
-            collective_id=0, has_side_effects=True, vmem_limit_bytes=48 * 1024 * 1024
+            collective_id=0, has_side_effects=True, vmem_limit_bytes=60 * 1024 * 1024
         ),
         name="edge_block_backward",
     )(
@@ -457,7 +457,7 @@
         pairs,
         edge_inputs[0],
         node_cotangent[0],
-        rotations.reshape(L0 * L0 * EDGES // 128, 128),
+        rotations.reshape(L0 * L0, EDGES // 128, 128),
         targets,
         counts,
     )

time: 93.1 us -> 92.7 us (level)
  Pallas kernels: 83.4 us -> 84.6 us
    unnamed x10 -> x2, local copies, waits for them, and re-layouts: 4.99 us -> 3.21 us
    pallas_call x1, Pallas kernels: 83.4 us -> 84.6 us  [per_device(): pl.pallas_call(kernel, out_shape=(jax.ShapeDtypeStruct((EDGES, K), BF16),...]
    unnamed x1 -> x0, other arithmetic: 1.14 us -> none
where the time goes in v3:
time: 92.7 us; the launch traced here: 92.3 us
  Pallas kernels  84.6 us (91%)
  local copies, waits for them, and re-layouts  5.62 us (6%)
  between operations  1.36 us (1%)
    pallas_call x1, Pallas kernels, per_device(): pl.pallas_call(kernel, out_shape=(jax.ShapeDtypeStruct((EDGES, K), BF16),...  84.6 us
    unnamed x2, local copies, waits for them, and re-layouts  3.21 us

profile of v3, /device:TPU:7, one launch (start us, length us, event | category | flops | bytes accessed | tf_op | source)
XLA Modules:
  0.0 92.3 jit_solution(13183860887934335901)
XLA Ops:
  1.3 1.0 %copy.9 = f32[1024,16]{1,0:T(8,128)S(1)} copy(f32[1024,16]{0,1:T(8,128)} %param.8) | data formatting | bytes 131072 | tf_op args[1]
  2.4 0.6 dynamic-slice_bitcast_fusion.coef_ref
  3.0 0.1 copy.11
  3.1 0.1 copy.13
  3.2 0.1 copy.10
  3.2 0.1 maximum_bitcast_fusion
  3.3 0.6 pad_maximum_fusion.ct_ref
  3.9 84.6 %edge_block_backward.1 = (bf16[512,896]{1,0:T(8,128)(2,1)}, f32[14,16,128]{2,1,0:T(8,128)}) custom-call(bf16[8,112,896]{2,1,0:T(8,128)(2,1)} %bitcast.24, f32[64,16]{1,0:T(8,128)} %dynamic-slice_bitcast_fusion.coef_ref, f32[2,16,16]{2,1,0:T(8,128)} %pad_maximum_fusion.ct_ref, bf16[512,896]{1,0:T(8,128)(2,1)} %bitcast.26, bf16[128,896]{1,0:T(8,128)(2,1)} %bitcast.29, ...), custom_call_target="tpu_custom_call" | custom-call | tf_op jit(solution)/shard_map/edge_block_backward/pallas_call | solution.py:410
  88.5 1.6 %slice_bitcast_fusion = f32[16,56,14]{1,0,2:T(8,128)} fusion(f32[14,16,128]{2,1,0:T(8,128)} %get-tuple-element.5), kind=kLoop, calls=%fused_computation | loop fusion | bytes 100352 | tf_op jit(solution)/shard_map/transpose | solution.py:464
  90.1 2.2 %copy.16 = bf16[1,512,896]{2,1,0:T(8,128)(2,1)} copy(bf16[1,512,896]{2,1,0:T(8,128)(2,1)} %bitcast.25) | data formatting | bytes 1835008
  (1 shorter events, 0.0 us)
